TPU v7x, 256 devices: a whole 4x4x8 slice. The times are simulated.
256 devices in a mesh: ctx: 32 (over z_lo, x, y), tp: 8 (over z_hi, core).
Axes of the slice: x: 4, y: 4, z: 8 (z_hi: 4, z_lo: 2; z = z_hi * 2 + z_lo), core: 2. Of those that a mesh axis runs over, the one named last changes fastest.
Arguments:
- residual: bfloat16 [8192, 8192], P('ctx', 'tp'), may hold values from -6 to 6
- streams: bfloat16 [8192, 3, 4096], P('ctx', None, 'tp'), may hold values from -6 to 6
- short_filter: bfloat16 [7, 3, 4096], P(None, None, 'tp'), may hold values from -2 to 2
- medium_filter: bfloat16 [128, 256], P(None, 'tp'), may hold values from -0.5 to 0.5
- queries: bfloat16 [8192, 4096], P('ctx', 'tp'), may hold values from -150 to 150
- keys: bfloat16 [8192, 4096], P('ctx', 'tp'), may hold values from -5 to 5
- values: bfloat16 [8192, 4096], P('ctx', 'tp'), may hold values from -6 to 6
- lengths: int32 [8], replicated, may hold values from 1 to 4352, 8192 in all
- w_out: bfloat16 [4096, 8192], P('tp'), may hold values from -0.125 to 0.125
Outputs:
- hyena_mix: bfloat16 [8192, 4096], P('ctx', 'tp')
- attended: bfloat16 [8192, 4096], P('ctx', 'tp')
- mixed: bfloat16 [8192, 8192], P('ctx', 'tp')
Inputs may be any that keep to these rules, and one draw needn't show every extreme that they name: `lengths`: each genome has at least one base, they cover the pack, and one genome has exactly 4352 bases.
All inputs are finite; a program needn't handle non-finite values.
Results may differ from a plain program's by a relative error of at most 0.012.
Values may be sent and summed in bfloat16 or wider, within the bound.
A program may use at most 192 MiB of HBM per device.

v0:
```python
import jax
import jax.numpy as jnp
from jax import lax
from jax.sharding import PartitionSpec as P

HD = 128


def shifted(value, axis, steps):
    count = lax.axis_size(axis)
    first, last = (max(0, -steps), min(count, count - steps))
    return lax.ppermute(value, axis, [(source, source + steps) for source in range(first, last)])


def genome_of(lengths, positions):
    ends = jnp.cumsum(lengths)
    return jnp.sum((ends[None, :] <= positions[:, None]).astype(jnp.int32), axis=1)


def body(residual, streams, short_filter, medium_filter, queries, keys, values, lengths, w_out):
    row_count = streams.shape[0]
    tap_count = short_filter.shape[0]
    first_row = lax.axis_index("ctx") * row_count
    offsets = jnp.arange(row_count, dtype=jnp.int32)
    arrived_rows = shifted(streams[row_count - (tap_count - 1) :], "ctx", 1)
    extended = jnp.concatenate([arrived_rows, streams], axis=0)
    genome_ext = genome_of(
        lengths,
        first_row - (tap_count - 1) + jnp.arange(row_count + tap_count - 1, dtype=jnp.int32),
    )
    genome_here = genome_ext[tap_count - 1 :]
    featured = jnp.zeros(streams.shape, jnp.float32)
    for lag_index in range(tap_count):
        start_row = tap_count - 1 - lag_index
        same_genome = genome_ext[start_row : start_row + row_count] == genome_here
        term = (
            extended[start_row : start_row + row_count].astype(jnp.float32)
            * short_filter[lag_index].astype(jnp.float32)[None]
        )
        featured = featured + jnp.where(same_genome[:, None, None], term, 0.0)
    featured = featured.astype(jnp.bfloat16)
    product = (featured[:, 1].astype(jnp.float32) * featured[:, 2].astype(jnp.float32)).astype(
        jnp.bfloat16
    )
    block_size = 128
    group_count = medium_filter.shape[1]
    group_width = product.shape[1] // group_count
    block_count = row_count // block_size
    product_prev = shifted(product[row_count - block_size :], "ctx", 1)
    genome_prod = genome_of(
        lengths, first_row - block_size + jnp.arange(row_count + block_size, dtype=jnp.int32)
    )
    genome_now = genome_prod[block_size:].reshape(block_count, block_size)
    genome_before = genome_prod[:row_count].reshape(block_count, block_size)
    current = product.reshape(block_count, block_size, group_count, group_width)
    earlier = jnp.concatenate([product_prev, product[: row_count - block_size]], axis=0).reshape(
        block_count, block_size, group_count, group_width
    )
    block_index = jnp.arange(block_size, dtype=jnp.int32)
    lag_table = (block_index[:, None] - block_index[None, :]) % block_size
    one_hot = (block_index[:, None, None] == lag_table[None]).astype(jnp.bfloat16)
    toeplitz = jnp.einsum(
        "lts,lg->gts", one_hot, medium_filter, preferred_element_type=jnp.float32
    ).astype(jnp.bfloat16)
    causal = block_index[:, None] >= block_index[None, :]
    zero_tile = jnp.zeros((), jnp.bfloat16)
    lower = jnp.where(causal[None], toeplitz, zero_tile)
    upper = jnp.where(causal[None], zero_tile, toeplitz)
    same_now = genome_now[:, :, None] == genome_now[:, None, :]
    same_prev = genome_now[:, :, None] == genome_before[:, None, :]
    near_part = jnp.where(same_now[:, None], lower[None], zero_tile)
    far_part = jnp.where(same_prev[:, None], upper[None], zero_tile)
    medium = jnp.einsum("bgts,bsgc->btgc", near_part, current, preferred_element_type=jnp.float32)
    medium = medium + jnp.einsum(
        "bgts,bsgc->btgc", far_part, earlier, preferred_element_type=jnp.float32
    )
    medium = medium.reshape(row_count, group_count * group_width)
    hyena_mix = (featured[:, 0].astype(jnp.float32) * medium).astype(jnp.bfloat16)
    head_width = queries.shape[1]
    head_count = head_width // HD
    score_scale = float(HD) ** (-0.5)
    query_heads = queries.reshape(row_count, head_count, HD)
    query_pos = first_row + offsets
    key_value = jnp.stack([keys, values])
    pieces = lax.all_gather(key_value, "ctx", axis=1, tiled=True)
    running_max = jnp.full((head_count, row_count), -1e30, jnp.float32)
    key_count = pieces.shape[1]
    key_pos = jnp.arange(key_count, dtype=jnp.int32)
    key_genome = genome_of(lengths, key_pos)
    allowed = (
        (key_pos[None, :] <= query_pos[:, None])
        & (key_genome[None, :] == genome_here[:, None])
        & (key_pos[None, :] >= 0)
    )
    scores = (
        jnp.einsum(
            "qhd,khd->hqk",
            query_heads,
            pieces[0].reshape(key_count, head_count, HD),
            preferred_element_type=jnp.float32,
        )
        * score_scale
    )
    scores = jnp.where(allowed[None], scores, -1e30)
    new_max = jnp.maximum(running_max, jnp.max(scores, axis=2))
    exps = jnp.where(allowed[None], jnp.exp(scores - new_max[:, :, None]), 0.0)
    running_sum = jnp.sum(exps, axis=2)
    gathered = jnp.einsum(
        "hqk,khd->qhd",
        exps.astype(jnp.bfloat16),
        pieces[1].reshape(key_count, head_count, HD),
        preferred_element_type=jnp.float32,
    )
    weighted = gathered
    running_max, running_sum, weighted = (new_max, running_sum, weighted)
    attended = (
        (weighted / jnp.transpose(running_sum)[:, :, None])
        .reshape(row_count, head_width)
        .astype(jnp.bfloat16)
    )
    partial_sum = jnp.dot(attended, w_out, preferred_element_type=jnp.float32)
    summed = lax.psum_scatter(
        partial_sum.astype(jnp.bfloat16), "tp", scatter_dimension=1, tiled=True
    ).astype(jnp.float32)
    mixed = (residual.astype(jnp.float32) + summed).astype(jnp.bfloat16)
    return (hyena_mix, attended, mixed)


def solution(mesh):
    in_specs = (
        P("ctx", "tp"),
        P("ctx", None, "tp"),
        P(None, None, "tp"),
        P(None, "tp"),
        P("ctx", "tp"),
        P("ctx", "tp"),
        P("ctx", "tp"),
        P(),
        P("tp", None),
    )
    out_specs = (P("ctx", "tp"), P("ctx", "tp"), P("ctx", "tp"))
    return jax.shard_map(body, mesh=mesh, in_specs=in_specs, out_specs=out_specs, check_vma=False)
```

profile of v0, /device:TPU:1, one launch (start us, length us, event | category | flops | bytes accessed | tf_op | source)
XLA Modules:
  0.0 400.1 jit_solution(1958808021990980428)
XLA Ops:
  7.2 1.1 copy.42
  8.4 1.1 copy.43
  9.5 0.8 pad_maximum_fusion.1
  10.9 3.8 fusion.7
  14.7 228.4 %all-gather.2.cloned.1.call-done = bf16[2,8192,512]{1,2,0:T(8,128)(2,1)} async-done(((bf16[2,256,512]{1,2,0:T(8,128)(2,1)}), bf16[2,8192,512]{1,2,0:T(8,128)(2,1)}) %all-gather.2.cloned.1.call-update) | async-done | bytes 16777232 | tf_op jit(solution)/shard_map/all_gather | solution.py:85
  243.0 11.6 %fusion.56 = (bf16[1,8192,512]{1,2,0:T(8,128)(2,1)}, bf16[1,8192,512]{1,2,0:T(8,128)(2,1)}) fusion(bf16[2,8192,512]{1,2,0:T(8,128)(2,1)} %all-gather.2.cloned.1.call-done), kind=kLoop, calls=%fused_computation.108 | loop fusion | bytes 33554432 | tf_op jit(solution)/shard_map/slice | solution.py:99
  254.6 16.2 %fusion = (f32[4,256]{1,0:T(4,128)S(1)}, f32[4,8192,256]{2,1,0:T(8,128)}) fusion(pred[256,8192]{0,1:T(8,128)(4,1)S(1)} %fusion.7, bf16[8192,4,128]{0,2,1:T(8,128)(2,1)} %bitcast.96, bf16[256,512]{1,0:T(8,128)(2,1)S(1)} %copy-done), kind=kOutput, calls=%fused_computation.2 | convolution fusion | flops 2172648448 | bytes 44306432 | tf_op jit(solution)/shard_map/qhd,khd->hqk/dot_general | solution.py:96
  270.8 15.0 %fusion.1 = f32[4,256]{1,0:T(4,128)S(1)} fusion(f32[4,8192,256]{2,1,0:T(8,128)} %get-tuple-element.36, f32[4,256]{1,0:T(4,128)S(1)} %broadcast_maximum_fusion, pred[256,8192]{0,1:T(8,128)(4,1)S(1)} %fusion.7), kind=kLoop, calls=%fused_computation.3 | loop fusion | flops 41942016 | bytes 35659776 | tf_op jit(solution)/shard_map/reduce_sum | solution.py:107
  285.8 20.7 %fusion.28 = bf16[256,4,128]{0,2,1:T(8,128)(2,1)S(1)} fusion(bf16[8192,4,128]{0,2,1:T(8,128)(2,1)} %bitcast.95, f32[4,8192,256]{2,1,0:T(8,128)} %get-tuple-element.36, f32[4,256]{1,0:T(4,128)S(1)} %broadcast_maximum_fusion, pred[256,8192]{0,1:T(8,128)(4,1)S(1)} %fusion.7, f32[256,4]{0,1:T(4,128)S(1)} %bitcast.106), kind=kOutput, calls=%fused_computation.35 | convolution fusion | flops 2189688832 | bytes 44310528 | tf_op jit(solution)/shard_map/hqk,khd->qhd/dot_general | solution.py:108
  306.5 7.7 %convolution_convert_fusion = bf16[256,8192]{1,0:T(8,128)(2,1)} fusion(bf16[256,512]{0,1:T(8,128)(2,1)S(1)} %bitcast.98, bf16[512,8192]{1,0:T(8,128)(2,1)} %param.17), kind=kOutput, calls=%fused_computation.7 | convolution fusion | flops 2149580800 | bytes 12845056 | tf_op jit(solution)/shard_map/dot_general | solution.py:121
  314.3 1.1 copy-done.2
  315.4 1.0 copy.35
  316.3 5.3 %collective-permute-start = (bf16[6,3,512]{0,2,1:T(8,128)(2,1)}, bf16[6,3,512]{0,2,1:T(8,128)(2,1)}, u32[]{:S(2)}, u32[]{:S(2)}) collective-permute-start(bf16[6,3,512]{0,2,1:T(8,128)(2,1)} %copy.35), channel_id=1, source_target_pairs={{0,8},{8,16},{16,24},{24,32},{32,40},{40,48},{48,56},{56,64},{64,7... | collective-permute-start | bytes 55304 | tf_op jit(solution)/shard_map/ppermute | solution.py:12
  322.0 2.9 select_bitcast_fusion
  325.3 2.6 copy.39
  327.9 1.4 copy.37
  329.3 6.3 %add_convert_fusion = bf16[256,3,512]{0,2,1:T(8,128)(2,1)S(1)} fusion(bf16[256,3,512]{0,2,1:T(8,128)(2,1)S(1)} %copy.34, bf16[6,3,512]{0,2,1:T(8,128)(2,1)} %collective-permute-done, f32[3,512]{1,0:T(4,128)S(1)} %get-tuple-element.37, f32[3,512]{1,0:T(4,128)S(1)} %get-tuple-element.38, f32[3,512]{1,0:T(4,128)S(1)} %get-tuple-element.39, ...), kind=kLoop, calls=%fused_computation.24 | loop fusion | flops 17694720 | bytes 1635840 | tf_op jit(solution)/shard_map/convert_element_type | solution.py:41
  335.8 1.5 collective-permute-start.1
  337.3 2.4 fusion.11
  340.4 2.4 fusion.19
  343.3 0.8 copy.47
  344.1 0.8 copy.48
  345.0 46.2 %reduce-scatter.2.cloned.1.call-done = bf16[256,1024]{1,0:T(8,128)(2,1)} async-done(((bf16[256,8192]{1,0:T(8,128)(2,1)}), bf16[256,1024]{1,0:T(8,128)(2,1)}) %reduce-scatter.2.cloned.1.call-update) | async-done | bytes 524304 | tf_op jit(solution)/shard_map/reduce_scatter | solution.py:122
  391.2 2.0 add_convert_fusion.1
  (47 shorter events, 2.6 us)
Async XLA Ops:
  7.2 247.4 %copy-start = (bf16[256,512]{1,0:T(8,128)(2,1)S(1)}, bf16[256,512]{1,0:T(8,128)(2,1)}, u32[]{:S(2)}) copy-start(bf16[256,512]{1,0:T(8,128)(2,1)} %param.13) | copy-start | bytes 786436
  7.2 3.2 copy-start.6
  7.2 235.8 %all-gather.2.cloned.1.call-start = ((), (), s32[]{:S(2)}) async-start(), calls=%async_computation.1 | async-start | bytes 17301504 | tf_op jit(solution)/shard_map/all_gather | solution.py:85
  10.3 380.9 %reduce-scatter.2.cloned.1.call-start = ((), (), s32[]{:S(2)}) async-start(), calls=%async_computation.2 | async-start | bytes 4718592 | tf_op jit(solution)/shard_map/reduce_scatter | solution.py:122
  314.2 1.1 copy-start.2
  314.2 7.5 %copy-start.4 = (bf16[7,3,512]{2,0,1:T(8,128)(2,1)S(1)}, bf16[7,3,512]{2,0,1:T(8,128)(2,1)}, u32[]{:S(2)}) copy-start(bf16[7,3,512]{2,0,1:T(8,128)(2,1)} %param.11) | copy-start | bytes 64516
  314.2 7.7 %copy-start.5 = (bf16[128,32]{0,1:T(8,128)(2,1)S(1)}, bf16[128,32]{0,1:T(8,128)(2,1)}, u32[]{:S(2)}) copy-start(bf16[128,32]{0,1:T(8,128)(2,1)} %param.12) | copy-start | bytes 24580
  316.3 13.0 %collective-permute-start = (bf16[6,3,512]{0,2,1:T(8,128)(2,1)}, bf16[6,3,512]{0,2,1:T(8,128)(2,1)}, u32[]{:S(2)}, u32[]{:S(2)}) collective-permute-start(bf16[6,3,512]{0,2,1:T(8,128)(2,1)} %copy.35), channel_id=1, source_target_pairs={{0,8},{8,16},{16,24},{24,32},{32,40},{40,48},{48,56},{56,64},{64,7... | collective-permute-start | bytes 55304 | tf_op jit(solution)/shard_map/ppermute | solution.py:12
  335.8 4.5 %collective-permute-start.1 = (bf16[128,512]{0,1:T(8,128)(2,1)S(1)}, bf16[128,512]{0,1:T(8,128)(2,1)S(1)}, u32[]{:S(2)}, u32[]{:S(2)}) collective-permute-start(bf16[128,512]{0,1:T(8,128)(2,1)S(1)} %get-tuple-element.16), channel_id=1, source_target_pairs={{0,8},{8,16},{16,24},{24,32},{32,40},{40,48},{48,56},{56,64},{64,7... | collective-permute-start | bytes 393224 | tf_op jit(solution)/shard_map/ppermute | solution.py:12
  342.8 48.4 %copy-start.3 = (bf16[256,1024]{1,0:T(8,128)(2,1)S(1)}, bf16[256,1024]{1,0:T(8,128)(2,1)}, u32[]{:S(2)}) copy-start(bf16[256,1024]{1,0:T(8,128)(2,1)} %param.9) | copy-start | bytes 1572868
  342.8 50.5 %copy-start.1 = (bf16[256,512]{1,0:T(8,128)(2,1)S(1)}, bf16[256,512]{1,0:T(8,128)(2,1)}, u32[]{:S(2)}) copy-start(bf16[256,512]{1,0:T(8,128)(2,1)} %param.13) | copy-start | bytes 786436
Sparse Core Ops, SparseCore 0:
  10.4 232.5 all-gather.1
  314.4 76.7 reduce-scatter.1
where the time goes:
time: 402 us; the launch traced here: 400 us
  waiting for transfers between devices  275 us (68%)
  matrix products  52.4 us (13%)
  other arithmetic  28.8 us (7%)
  local copies, waits for them, and re-layouts  22.5 us (6%)
  between operations  14.3 us (4%)
  starting transfers between devices  6.85 us (2%)
    all_gather x1, waiting for transfers between devices, body(): pieces = lax.all_gather(key_value, 'ctx', axis=1, tiled=True)  228 us
    reduce_scatter x1, waiting for transfers between devices, body(): lax.psum_scatter(partial_sum.astype(jnp.bfloat16), 'tp', scatter_dimensio...  46.2 us
    dot_general x1, matrix products, body(): jnp.einsum('hqk,khd->qhd', exps.astype(jnp.bfloat16), pieces[1].reshape(k...  20.7 us
    dot_general x1, matrix products, body(): jnp.einsum('qhd,khd->hqk', query_heads, pieces[0].reshape(key_count, head...  16.2 us
    reduce_sum x1, other arithmetic, body(): running_sum = jnp.sum(exps, axis=2)  15 us
    slice x1, local copies, waits for them, and re-layouts, body(): pieces[0].reshape(key_count, head_count, HD)  11.6 us
  transfers between devices with their start and end apart: 4, of which 3 were waited for; matrix products, arithmetic and copies ran while one was open for 7% of the time, Pallas kernels for 0%

commit v1 on v0

v1 whole, which is shorter than its diff:
```python
import functools
import math

import jax
import jax.numpy as jnp
from jax import lax
from jax.experimental import pallas as pl
from jax.experimental.pallas import tpu as pltpu
from jax.sharding import PartitionSpec as P

HD = 128
ROWS = 256
GENOMES = 8
SHORT = 7
WIDE = 512
COLS = 1024
START = -1.0e30
NEVER = -2.0e30
LOG2 = math.log2(math.e) / math.sqrt(HD)
MESH = pl.DeviceIdType.MESH


def iota(shape, axis):
    return lax.broadcasted_iota(jnp.int32, shape, axis)


def kernel(
    lengths, residual, streams, short, medium, queries, keys, values, w_out,
    hyena, attended, mixed,
    qb, kb, vb, vt, gq, gk, mst, lst, acc, oth, ost, ob, att, wb, snd, rcv, res, mix,
    sb, f0, prod, hyo, lo_sem,
    a_send, a_recv, g_send, g_recv, h_send, h_recv, z_send, z_recv, r_send, r_recv,
    o_send, o_recv, w_send, w_recv, p_send, p_recv, n_send, n_recv,
):
    c, t = lax.axis_index("ctx"), lax.axis_index("tp")
    z, x, y = c // 16, lax.rem(c // 4, 4), lax.rem(c, 4)
    zh, p = t // 2, lax.rem(t, 2)
    a, b = x + (y - x) * p, y + (x - y) * p
    sa, sb_ = 4 - 3 * p, 1 + 3 * p

    def ring(v, d):
        return lax.rem(v + d, 4)

    def dev(a1, b1):
        return (16 * z + a1 * sa + b1 * sb_, t)

    def tile(a1, b1):
        return a1 * sa + b1 * sb_

    left, right = dev(a, ring(b, 3)), dev(a, ring(b, 1))
    across = (lax.rem(c + 16, 32), t)
    sibling = (c, t + 1 - 2 * p)
    up, down = (c, lax.rem(t + 2, 8)), (c, lax.rem(t + 6, 8))
    after, before = (lax.rem(c + 1, 32), t), (lax.rem(c + 31, 32), t)

    def remote(src, dst, send, recv, to):
        return pltpu.make_async_remote_copy(
            src_ref=src, dst_ref=dst, send_sem=send, recv_sem=recv, device_id=to, device_id_type=MESH
        )

    def head(ref, h):
        return ref.at[:, pl.ds(pl.multiple_of(h * HD, HD), HD)]

    me = tile(a, b)
    own = [
        pltpu.make_async_copy(head(keys, a), kb.at[me], lo_sem.at[0]),
        pltpu.make_async_copy(head(values, a), vb.at[me], lo_sem.at[1]),
        pltpu.make_async_copy(head(queries, a), qb.at[a], lo_sem.at[2]),
    ]
    for copy in own:
        copy.start()
    streams_in = pltpu.make_async_copy(streams, sb.at[:, pl.ds(16, ROWS)], lo_sem.at[3])
    streams_in.start()
    residual_in = pltpu.make_async_copy(residual, res, lo_sem.at[4])

    def block_cols(j, parity):
        return w_out.at[:, pl.ds(pl.multiple_of((2 * j + parity) * COLS, COLS), COLS)]

    weights_in = [
        pltpu.make_async_copy(block_cols(j, p), wb.at[p, j], lo_sem.at[5 + j]) for j in range(4)
    ]

    barrier = pltpu.get_barrier_semaphore()
    partners = [dev(ring(a, d), b) for d in (1, 2, 3)] + [
        left, right, across, sibling, up, down, after, before,
    ]
    for to in partners:
        pl.semaphore_signal(barrier, inc=1, device_id=to, device_id_type=MESH)
    pl.semaphore_wait(barrier, len(partners))

    def spread(d, i):
        to_a = ring(a, d)
        src = (keys, values, queries)[i]
        dst = (kb.at[me], vb.at[me], qb.at[a])[i]
        return remote(head(src, to_a), dst, a_send.at[d, i], a_recv.at[d, i], dev(to_a, b))

    def spread_in(d, i):
        from_a = ring(a, 4 - d)
        dst = (kb.at[tile(from_a, b)], vb.at[tile(from_a, b)], qb.at[from_a])[i]
        return remote(dst, dst, a_send.at[d, i], a_recv.at[d, i], dev(from_a, b))

    for d in (1, 3, 2):
        for i in range(3):
            spread(d, i).start()
    halo = remote(
        streams.at[:, pl.ds(ROWS - 16, 16)], sb.at[:, pl.ds(0, 16)], h_send.at[0], h_recv.at[0], after
    )
    halo.start()
    swap = [
        remote(block_cols(j, 1 - p), wb.at[p, j], w_send.at[j], w_recv.at[j], sibling) for j in range(4)
    ]
    for copy in weights_in + swap + [residual_in]:
        copy.start()

    def gather(d, i, way):
        j = tile(ring(a, 4 - d), b)
        ref = (kb, vb)[i].at[j]
        to = right if way == 0 else left
        return remote(ref, ref, g_send.at[0, d, i, way], g_recv.at[0, d, i, way], to)

    def gather_in(d, i, way):
        j = tile(ring(a, 4 - d), ring(b, 3 if way == 0 else 1))
        ref = (kb, vb)[i].at[j]
        return remote(ref, ref, g_send.at[0, d, i, way], g_recv.at[0, d, i, way], left)

    def onward(d, i):
        j = tile(ring(a, 4 - d), ring(b, 3 if i == 0 else 1))
        ref = (kb, vb)[i].at[j]
        to = right if i == 0 else left
        return remote(ref, ref, g_send.at[1, d, i, 0], g_recv.at[1, d, i, 0], to)

    def onward_in(d, i):
        ref = (kb, vb)[i].at[tile(ring(a, 4 - d), ring(b, 2))]
        return remote(ref, ref, g_send.at[1, d, i, 0], g_recv.at[1, d, i, 0], left)

    def visit(d):
        i = ring(a, 4 - d)
        return remote(qb.at[i], qb.at[4 + i], z_send.at[d], z_recv.at[d], across)

    def pass_on(d):
        for i in range(2):
            for way in range(2):
                gather(d, i, way).start()

    for copy in own:
        copy.wait()
    pass_on(0)

    @pl.when(z == 1)
    def _():
        visit(0).start()
        qb[4:8] = jnp.zeros((4, ROWS, HD), jnp.bfloat16)

    starts, ends, total = [], [], jnp.int32(0)
    for j in range(GENOMES):
        starts.append(total)
        total = total + lengths[j]
        ends.append(total)
    lane = iota((1, HD), 1)
    first_of, end_of = jnp.zeros((1, HD), jnp.int32), jnp.zeros((1, HD), jnp.int32)
    for j in range(GENOMES):
        first_of = jnp.where(lane == j, starts[j], first_of)
        end_of = jnp.where(lane == j, ends[j], end_of)

    def inside(position):
        spot = position + iota((ROWS, HD), 0)
        return (spot >= first_of) & (spot < end_of)

    @pl.loop(0, 16)
    def _(j):
        gk[j] = jnp.where(inside((16 * z + j) * ROWS), 0.0, NEVER).astype(jnp.bfloat16)

    @pl.loop(0, 8)
    def _(i):
        j = tile(lax.rem(i, 4), b) + 16 * jnp.where(i >= 4, 1, z)
        gq[i] = jnp.where(inside(j * ROWS), 1.0, 0.0).astype(jnp.bfloat16)

    mst[...] = jnp.full(mst.shape, START, jnp.float32)
    lst[...] = jnp.zeros(lst.shape, jnp.float32)
    acc[...] = jnp.zeros(acc.shape, jnp.float32)

    for d in (1, 3, 2):
        spread_in(d, 0).wait_recv()
        spread_in(d, 1).wait_recv()
        pass_on(d)
        spread_in(d, 2).wait_recv()

        @pl.when(z == 1)
        def _():
            visit(d).start()

    streams_in.wait()
    halo.wait_recv()
    base = c * ROWS
    spot = base + iota((ROWS, HD), 0)
    first = jnp.zeros((ROWS, HD), jnp.int32)
    for j in range(1, GENOMES):
        first = jnp.where(spot >= starts[j], starts[j], first)
    depth = spot - first

    @pl.loop(0, 4)
    def _(n):
        lanes = pl.ds(pl.multiple_of(n * HD, HD), HD)
        made = []
        for j in range(3):
            data = sb[j, :, lanes].astype(jnp.float32)
            taps = short[j, :, lanes].astype(jnp.float32)
            total = data[16:] * taps[0:1]
            for lag in range(1, SHORT):
                moved = pltpu.roll(data, lag, 0)[16:]
                total = total + jnp.where(depth >= lag, moved * taps[lag : lag + 1], 0.0)
            made.append(total.astype(jnp.bfloat16))
        f0[n] = made[0]
        prod[n, pl.ds(128, ROWS)] = (
            made[1].astype(jnp.float32) * made[2].astype(jnp.float32)
        ).astype(jnp.bfloat16)

    tail = remote(
        prod.at[:, pl.ds(ROWS, 128)], prod.at[:, pl.ds(0, 128)], h_send.at[1], h_recv.at[1], after
    )
    tail.start()

    @pl.when(z == 0)
    def _():
        for d in range(4):
            i = ring(a, 4 - d)
            remote(qb.at[4 + i], qb.at[4 + i], z_send.at[d], z_recv.at[d], across).wait_recv()

    def attend(ks, ss, offs):
        scores = []
        for i in range(4):
            q = ss[i] if ss[i] is None else jnp.minimum(ss[i], 7)
            wide_k = jnp.concatenate([kb[ks[i]], gk[ks[i]]], axis=1)
            wide_q = jnp.concatenate([qb[q], gq[q]], axis=1)
            s = lax.dot_general(
                wide_k, wide_q, (((1,), (1,)), ((), ())), preferred_element_type=jnp.float32
            )
            if offs is not None:
                ahead = iota((ROWS, ROWS), 0) - iota((ROWS, ROWS), 1)
                s = jnp.where(ahead <= offs[i], s, NEVER)
            scores.append(s)
        old = [mst[ss[i]] for i in range(4)]
        new = [
            jnp.maximum(old[i], jnp.max(scores[i], axis=0, keepdims=True)) for i in range(4)
        ]
        exps = [jnp.exp2(scores[i] * LOG2 - new[i][0:1] * LOG2) for i in range(4)]
        fade = [jnp.exp2((old[i] - new[i]) * LOG2) for i in range(4)]
        sums = [
            lst[ss[i]] * fade[i] + jnp.sum(exps[i].reshape(ROWS // 8, 8, ROWS), axis=0)
            for i in range(4)
        ]
        outs = [
            acc[ss[i]] * fade[i][0:1]
            + jnp.dot(vt[ks[i]], exps[i].astype(jnp.bfloat16), preferred_element_type=jnp.float32)
            for i in range(4)
        ]
        for i in range(4):
            mst[ss[i]] = new[i]
            lst[ss[i]] = sums[i]
            acc[ss[i]] = outs[i]

    slots = [tile(i, b) for i in range(4)]

    def turn(j):
        vt[j] = vb[j].astype(jnp.float32).T.astype(jnp.bfloat16)

    @pl.loop(0, 5)
    def _(n):
        d = jnp.minimum(n, 3)
        j = tile(ring(a, 4 - d), b)

        @pl.when(n < 4)
        def _():
            turn(j)

        ks = [jnp.where(n < 4, j, slots[i]) for i in range(4)]
        ss = [i + 4 * jnp.where((n == 4) | (j > slots[i]), 1, 0) for i in range(4)]
        offs = [
            jnp.where(ss[i] >= 4, ROWS, (slots[i] - ks[i]) * ROWS) for i in range(4)
        ]
        attend(ks, ss, offs)

    @pl.loop(0, 13)
    def _(n):
        near = n < 8
        d = jnp.where(near, n // 2, jnp.minimum(n, 11) - 8)
        side = jnp.where(near, 3 - 2 * lax.rem(n, 2), 2)
        j = tile(ring(a, 4 - d), ring(b, side))

        @pl.when(near & (side == 3))
        def _():
            gather_in(d, 0, 0).wait_recv()
            onward(d, 0).start()
            gather_in(d, 1, 0).wait_recv()

        @pl.when(near & (side == 1))
        def _():
            gather_in(d, 1, 1).wait_recv()
            onward(d, 1).start()
            gather_in(d, 0, 1).wait_recv()

        @pl.when((n >= 8) & (n < 12))
        def _():
            onward_in(d, 0).wait_recv()
            onward_in(d, 1).wait_recv()

        @pl.when(n < 12)
        def _():
            turn(j)

        last = n == 12
        ks = [jnp.where(last, jnp.maximum(slots[i] - 1, 0), j) for i in range(4)]
        ss = [
            jnp.where(
                last & (slots[i] == 0), 8, i + 4 * jnp.where(last | (j > slots[i]), 1, 0)
            )
            for i in range(4)
        ]
        attend(ks, ss, None)

    def give(i):
        return [
            remote(oth.at[0, i], oth.at[1, i], r_send.at[0, i], r_recv.at[0, i], across),
            remote(ost.at[0, i], ost.at[1, i], r_send.at[1, i], r_recv.at[1, i], across),
        ]

    def close(i):
        total = jnp.sum(lst[i], axis=0, keepdims=True)
        return total, acc[i] / jnp.maximum(total, 1.0e-30)

    @pl.when(z == 0)
    def _():
        for i in range(4):
            total, out = close(4 + i)
            oth[0, i] = out.astype(jnp.bfloat16)
            ost[0, i, 0] = mst[4 + i]
            ost[0, i, 1] = jnp.broadcast_to(total, (8, ROWS))
            for copy in give(i):
                copy.start()

    def home(d):
        to_a = ring(a, d)
        return remote(ob.at[to_a], att.at[p, a], o_send.at[d], o_recv.at[d], dev(to_a, b))

    def home_in(d):
        ref = att.at[p, ring(a, 4 - d)]
        return remote(ref, ref, o_send.at[d], o_recv.at[d], dev(ring(a, 4 - d), b))

    for d in (1, 2, 3, 0):
        i = ring(a, d)
        total, out = close(i)
        ob[i] = out.T.astype(jnp.bfloat16)

        @pl.when(z == 1)
        def _():
            for copy in give(i):
                copy.wait_recv()
            m_other, l_other = ost[1, i, 0, 0:1], ost[1, i, 1, 0:1]
            m_own = mst[i, 0:1]
            top = jnp.maximum(m_own, m_other)
            w_own = jnp.exp2((m_own - top) * LOG2) * total
            w_other = jnp.exp2((m_other - top) * LOG2) * l_other
            both = (out * w_own + oth[1, i].astype(jnp.float32) * w_other) / (w_own + w_other)
            ob[i] = both.T.astype(jnp.bfloat16)

        if d > 0:
            home(d).start()
        else:
            att[p, a] = ob[i]
    for d in (1, 2, 3):
        home_in(d).wait_recv()
    cross = remote(att.at[p], att.at[p], n_send.at[0], n_recv.at[0], sibling)
    cross.start()
    attended_out = [
        pltpu.make_async_copy(att.at[p, i], head(attended, i), lo_sem.at[9 + i]) for i in range(4)
    ]
    for copy in attended_out:
        copy.start()
    rcv[:, 0] = jnp.zeros((2, 2, 128, WIDE), jnp.bfloat16)
    for copy in weights_in:
        copy.wait()
    for j in range(4):
        remote(wb.at[1 - p, j], wb.at[1 - p, j], w_send.at[j], w_recv.at[j], sibling).wait_recv()
    residual_in.wait()
    tail.wait_recv()
    cross_in = remote(att.at[1 - p], att.at[1 - p], n_send.at[0], n_recv.at[0], sibling)
    cross_in.wait_recv()

    def sum_step(step, half, way):
        return remote(
            snd.at[way, step, half], rcv.at[way, step + 1, half],
            p_send.at[way, step, half], p_recv.at[way, step + 1, half], (up, down)[way],
        )

    def sum_in(step, half, way):
        ref = rcv.at[way, step, half]
        return remote(ref, ref, p_send.at[way, 0, half], p_recv.at[way, step, half], (down, up)[way])

    flip = jnp.where(
        lax.rem(iota((128, 128), 0) + iota((128, 128), 1), 128) == 0, 1.0, 0.0
    ).astype(jnp.bfloat16)
    taps_back = jnp.dot(medium[...], flip, preferred_element_type=jnp.float32)
    hyo_taps = taps_back

    def genome_at(position):
        genome = jnp.zeros(position.shape, jnp.int32)
        for j in range(GENOMES):
            genome = genome + jnp.where(position >= ends[j], 1, 0)
        return genome

    mst[0:4, :, 0:128] = hyo_taps.reshape(4, 8, 128)

    def convolve(n):
        lt, blk = n // 2, lax.rem(n, 2)
        here = base + blk * 128
        rows, cols = iota((128, 128), 0), iota((128, 128), 1)
        genome_now = genome_at(here + rows)
        genome_src = genome_at(here + cols)
        earlier = here - 128 + cols
        genome_prev = genome_at(earlier)
        near = (genome_now == genome_src) & (rows >= cols)
        far = (genome_now == genome_prev) & (rows < cols) & (earlier >= 0)
        data = prod[lt, pl.ds(pl.multiple_of(blk * 128, 128), 256)]
        band = iota((128, 128), 1) // 16
        out = jnp.zeros((128, 128), jnp.float32)
        for g in range(8):
            taps = jnp.broadcast_to(mst[lt, g : g + 1, 0:128], (128, 128))
            around = pltpu.roll(taps, 0, 1, stride=1, stride_axis=0)
            weights = jnp.concatenate(
                [jnp.where(far, around, 0.0), jnp.where(near, around, 0.0)], axis=1
            ).astype(jnp.bfloat16)
            term = jnp.dot(weights, data, preferred_element_type=jnp.float32)
            out = jnp.where(band == g, term, out)
        place = pl.ds(pl.multiple_of(blk * 128, 128), 128)
        hyo[lt, place] = (f0[lt, place].astype(jnp.float32) * out).astype(jnp.bfloat16)

    @pl.loop(0, 8)
    def _(n):
        step, half = n // 2, lax.rem(n, 2)
        place = pl.ds(pl.multiple_of(half * 128, 128), 128)
        for way in range(2):
            j = ring(zh, 3 - step if way == 0 else 1 + step)
            part = jnp.zeros((128, WIDE), jnp.float32)
            for k in range(2):
                rows = jnp.concatenate([att[k, i, place] for i in range(4)], axis=1)
                part = part + jnp.dot(
                    rows, wb[k, j, :, way * WIDE : (way + 1) * WIDE],
                    preferred_element_type=jnp.float32,
                )

            @pl.when(step > 0)
            def _():
                sum_in(step, half, way).wait_recv()

            part = part + rcv[way, step, half].astype(jnp.float32)

            @pl.when(step < 3)
            def _():
                snd[way, step, half] = part.astype(jnp.bfloat16)
                sum_step(step, half, way).start()

            @pl.when(step == 3)
            def _():
                lanes = slice(way * WIDE, (way + 1) * WIDE)
                mix[place, lanes] = (
                    res[place, lanes].astype(jnp.float32) + part
                ).astype(jnp.bfloat16)

        convolve(n)

    outs = [
        pltpu.make_async_copy(hyo.at[i], head(hyena, i), lo_sem.at[i]) for i in range(4)
    ] + [pltpu.make_async_copy(mix, mixed, lo_sem.at[4])]
    for copy in outs:
        copy.start()

    for d in (1, 2, 3):
        for i in range(3):
            spread(d, i).wait_send()
        home(d).wait_send()
    halo.wait_send()
    tail.wait_send()
    cross.wait_send()
    for copy in swap:
        copy.wait_send()
    for d in range(4):
        for i in range(2):
            for way in range(2):
                gather(d, i, way).wait_send()
            onward(d, i).wait_send()

    @pl.when(z == 1)
    def _():
        for d in range(4):
            visit(d).wait_send()

    @pl.when(z == 0)
    def _():
        for i in range(4):
            for copy in give(i):
                copy.wait_send()

    for way in range(2):
        for step in range(3):
            for half in range(2):
                sum_step(step, half, way).wait_send()
    for copy in outs + attended_out:
        copy.wait()


def body(residual, streams, short_filter, medium_filter, queries, keys, values, lengths, w_out):
    bf16, f32 = jnp.bfloat16, jnp.float32
    anywhere = pl.BlockSpec(memory_space=pl.ANY)
    vmem = pl.BlockSpec(memory_space=pltpu.VMEM)
    dma = pltpu.SemaphoreType.DMA
    scratch = [
        pltpu.VMEM((8, ROWS, HD), bf16),
        pltpu.VMEM((16, ROWS, HD), bf16),
        pltpu.VMEM((16, ROWS, HD), bf16),
        pltpu.VMEM((16, HD, ROWS), bf16),
        pltpu.VMEM((8, ROWS, HD), bf16),
        pltpu.VMEM((16, ROWS, HD), bf16),
        pltpu.VMEM((9, 8, ROWS), f32),
        pltpu.VMEM((9, 8, ROWS), f32),
        pltpu.VMEM((9, HD, ROWS), f32),
        pltpu.VMEM((2, 4, HD, ROWS), bf16),
        pltpu.VMEM((2, 4, 2, 8, ROWS), f32),
        pltpu.VMEM((4, ROWS, HD), bf16),
        pltpu.VMEM((2, 4, ROWS, HD), bf16),
        pltpu.VMEM((2, 4, 512, COLS), bf16),
        pltpu.VMEM((2, 3, 2, 128, WIDE), bf16),
        pltpu.VMEM((2, 4, 2, 128, WIDE), bf16),
        pltpu.VMEM((ROWS, COLS), bf16),
        pltpu.VMEM((ROWS, COLS), bf16),
        pltpu.VMEM((3, ROWS + 16, 512), bf16),
        pltpu.VMEM((4, ROWS, HD), bf16),
        pltpu.VMEM((4, ROWS + 128, HD), bf16),
        pltpu.VMEM((4, ROWS, HD), bf16),
        dma((13,)),
        dma((4, 3)), dma((4, 3)),
        dma((2, 4, 2, 2)), dma((2, 4, 2, 2)),
        dma((2,)), dma((2,)),
        dma((4,)), dma((4,)),
        dma((2, 4)), dma((2, 4)),
        dma((4,)), dma((4,)),
        dma((4,)), dma((4,)),
        dma((2, 3, 2)), dma((2, 4, 2)),
        dma((1,)), dma((1,)),
    ]
    return pl.pallas_call(
        kernel,
        out_shape=(
            jax.ShapeDtypeStruct((ROWS, 512), bf16),
            jax.ShapeDtypeStruct((ROWS, 512), bf16),
            jax.ShapeDtypeStruct((ROWS, COLS), bf16),
        ),
        in_specs=[
            pl.BlockSpec(memory_space=pltpu.SMEM), anywhere, anywhere, vmem, vmem,
            anywhere, anywhere, anywhere, anywhere,
        ],
        out_specs=(anywhere, anywhere, anywhere),
        scratch_shapes=scratch,
        compiler_params=pltpu.CompilerParams(
            collective_id=0, has_side_effects=True, vmem_limit_bytes=56 * 1024 * 1024
        ),
        cost_estimate=pl.CostEstimate(
            flops=7_000_000_000, bytes_accessed=16_000_000, transcendentals=5_000_000
        ),
        name="mixer",
    )(
        lengths, residual, jnp.transpose(streams, (1, 0, 2)), jnp.transpose(short_filter, (1, 0, 2)),
        medium_filter.T, queries, keys, values, w_out,
    )


def solution(mesh):
    in_specs = (
        P("ctx", "tp"),
        P("ctx", None, "tp"),
        P(None, None, "tp"),
        P(None, "tp"),
        P("ctx", "tp"),
        P("ctx", "tp"),
        P("ctx", "tp"),
        P(),
        P("tp", None),
    )
    out_specs = (P("ctx", "tp"), P("ctx", "tp"), P("ctx", "tp"))
    return jax.shard_map(body, mesh=mesh, in_specs=in_specs, out_specs=out_specs, check_vma=False)
```

time: 402 us -> 91.2 us (0.23)
  the two profiles are of different devices: /device:TPU:1 before, /device:TPU:32 now
where the time goes in v1:
time: 91.2 us; the launch traced here: 90.9 us
  Pallas kernels  85.1 us (93%)
  local copies, waits for them, and re-layouts  5.21 us (6%)
    pallas_call x1, Pallas kernels, body(): pl.pallas_call(kernel, out_shape=(jax.ShapeDtypeStruct((ROWS, 512), bf16)...  85.1 us
    unnamed x3, local copies, waits for them, and re-layouts  5.21 us

profile of v1, /device:TPU:32, one launch (start us, length us, event | category | flops | bytes accessed | tf_op | source)
XLA Modules:
  0.0 90.9 jit_solution(6203111349712913761)
XLA Ops:
  0.6 85.1 %mixer.1 = (bf16[256,512]{1,0:T(8,128)(2,1)}, bf16[256,512]{1,0:T(8,128)(2,1)}, bf16[256,1024]{1,0:T(8,128)(2,1)}) custom-call(s32[8]{0:T(128)} %lengths.1, bf16[256,1024]{1,0:T(8,128)(2,1)} %residual.1, bf16[3,256,512]{2,1,0:T(8,128)(2,1)} %bitcast.3, bf16[3,7,512]{2,1,0:T(8,128)(2,1)} %bitcast.4, bf16[32,128]{1,0:T(8,128)(2,1)} %bitcast.5, ...), custom_call_target="tpu_custom_call" | custom-call | flops 7000000000 | bytes 16000000 | tf_op jit(solution)/shard_map/mixer/pallas_call | solution.py:550
  85.7 1.7 %copy.15 = bf16[256,512]{1,0:T(8,128)(2,1)} copy(bf16[256,512]{1,0:T(8,128)(2,1)} %get-tuple-element.6) | data formatting | bytes 524288
  87.4 1.7 %copy.16 = bf16[256,512]{1,0:T(8,128)(2,1)} copy(bf16[256,512]{1,0:T(8,128)(2,1)} %get-tuple-element.7) | data formatting | bytes 524288
  89.1 1.9 %copy.17 = bf16[256,1024]{1,0:T(8,128)(2,1)} copy(bf16[256,1024]{1,0:T(8,128)(2,1)} %get-tuple-element.8) | data formatting | bytes 1048576

commit v2 on v1

v2 whole, which is shorter than its diff:
```python
import functools
import math

import jax
import jax.numpy as jnp
from jax import lax
from jax.experimental import pallas as pl
from jax.experimental.pallas import tpu as pltpu
from jax.sharding import PartitionSpec as P

HD = 128
ROWS = 256
GENOMES = 8
SHORT = 7
WIDE = 512
COLS = 1024
START = -1.0e30
NEVER = -2.0e30
LOG2 = math.log2(math.e) / math.sqrt(HD)
MESH = pl.DeviceIdType.MESH
FAR = (0, 1)
EARLY = False
CONTROL = {"ls": {1: 8, 3: 9}, "lo": {1: 15, 3: 16}, "ps": {}}


def iota(shape, axis):
    return lax.broadcasted_iota(jnp.int32, shape, axis)


def kernel(
    lengths_in, residual, streams, short_in, medium_in, queries, keys, values, w_out,
    hyena, attended, mixed,
    lengths, short, medium, plain, tq, tv, qt, even, odd, kb, vt, gk, mst, lst, acc, oth, ost, ob, att, wb, sums, res, mix,
    taps_ref, sb, f0, prod, hyo, lo_sem,
    a_send, a_recv, g_send, g_recv, h_send, h_recv, z_send, z_recv, r_send, r_recv,
    o_send, o_recv, w_send, w_recv, s_send, s_recv, l_send, l_recv, m_send, m_recv,
    p_send, p_recv, n_send, n_recv,
):
    c, t = lax.axis_index("ctx"), lax.axis_index("tp")
    z, x, y = c // 16, lax.rem(c // 4, 4), lax.rem(c, 4)
    zh, p = t // 2, lax.rem(t, 2)
    a, b = x + (y - x) * p, y + (x - y) * p
    sa, sb_ = 4 - 3 * p, 1 + 3 * p

    def ring(v, d):
        return lax.rem(v + d, 4)

    def dev(a1, b1):
        return (16 * z + a1 * sa + b1 * sb_, t)

    def tile(a1, b1):
        return a1 * sa + b1 * sb_

    left, right = dev(a, ring(b, 3)), dev(a, ring(b, 1))
    across = (lax.rem(c + 16, 32), t)
    sibling = (c, t + 1 - 2 * p)
    after, before = (lax.rem(c + 1, 32), t), (lax.rem(c + 31, 32), t)

    def remote(src, dst, send, recv, to):
        return pltpu.make_async_remote_copy(
            src_ref=src, dst_ref=dst, send_sem=send, recv_sem=recv, device_id=to, device_id_type=MESH
        )

    def head(ref, h):
        return ref.at[:, pl.ds(pl.multiple_of(h * HD, HD), HD)]

    me = tile(a, b)
    both_in = [
        pltpu.make_async_copy(queries, plain.at[0], lo_sem.at[2]),
        pltpu.make_async_copy(values, plain.at[1], lo_sem.at[1]),
    ]
    small_in = [
        pltpu.make_async_copy(lengths_in, lengths, lo_sem.at[13]),
        pltpu.make_async_copy(short_in, short, lo_sem.at[14]),
        pltpu.make_async_copy(medium_in, medium, lo_sem.at[15]),
    ]
    own = pltpu.make_async_copy(head(keys, a), kb.at[me], lo_sem.at[0])
    for copy in both_in + small_in + [own]:
        copy.start()
    streams_in = pltpu.make_async_copy(streams, sb.at[:, pl.ds(16, ROWS)], lo_sem.at[3])
    streams_in.start()
    residual_in = pltpu.make_async_copy(residual, res, lo_sem.at[4])

    def block_cols(j, rows):
        return w_out.at[rows, :, pl.ds(pl.multiple_of(j * COLS, COLS), COLS)]

    every = pl.ds(0, 16)
    weights_in = pltpu.make_async_copy(block_cols(t, every), wb.at[0, p], lo_sem.at[5])
    over_z = [
        (c, lax.rem(2 * zh + 2 * d, 8) + core) for d in (1, 2, 3) for core in range(2)
    ]

    barrier = pltpu.get_barrier_semaphore()
    partners = [dev(ring(a, d), b) for d in (1, 2, 3)] + over_z + [
        left, right, across, sibling, after, before,
    ]
    for to in partners:
        pl.semaphore_signal(barrier, inc=1, device_id=to, device_id_type=MESH)
    for i, copy in enumerate(both_in):
        copy.wait()
        for h in range(4):
            turned = plain[i, :, h * HD : (h + 1) * HD].astype(jnp.float32).T
            (tq, tv)[i][h] = turned.astype(jnp.bfloat16)
    top = pl.ds(0, HD)
    qt[a, 0:HD] = tq[a]
    vt[me] = tv[a]
    pl.semaphore_wait(barrier, len(partners))

    def spread(d, i):
        to_a = ring(a, d)
        src = (head(keys, to_a), tv.at[to_a], tq.at[to_a])[i]
        dst = (kb.at[me], vt.at[me], qt.at[a, top])[i]
        return remote(src, dst, a_send.at[d, i], a_recv.at[d, i], dev(to_a, b))

    def spread_in(d, i):
        from_a = ring(a, 4 - d)
        dst = (kb.at[tile(from_a, b)], vt.at[tile(from_a, b)], qt.at[from_a, top])[i]
        return remote(dst, dst, a_send.at[d, i], a_recv.at[d, i], dev(from_a, b))

    for i in (2, 0, 1):
        for d in (1, 3, 2):
            spread(d, i).start()
    halo = remote(
        streams.at[:, pl.ds(ROWS - 16, 16)], sb.at[:, pl.ds(0, 16)], h_send.at[0], h_recv.at[0], after
    )
    halo.start()
    swap = remote(
        block_cols(t + 1 - 2 * p, every), wb.at[0, p], w_send.at[0], w_recv.at[0], sibling
    )

    def shard(d, core):
        spot = y * 4 + x + (x * 4 + y - y * 4 - x) * core
        to = lax.rem(2 * zh + 2 * d, 8) + core
        return remote(
            block_cols(to, spot), wb.at[4 - d, p, spot],
            s_send.at[d, core], s_recv.at[d, p], (c, to),
        )

    def shard_in(d, core):
        ref = wb.at[4 - d, core, 4 * b + a]
        return remote(ref, ref, s_send.at[d, core], s_recv.at[d, core], sibling)

    for d in (3, 1):
        for core in range(2):
            shard(d, core).start()

    def shards_start():
        for core in range(2):
            shard(2, core).start()
        for copy in (weights_in, swap, residual_in):
            copy.start()

    prev_a, next_a = dev(ring(a, 3), b), dev(ring(a, 1), b)
    pair = pl.ds(0, 2)

    def line(k, op):
        e, here = k, 4 * b
        ref = (
            wb.at[e, pair, here + a], wb.at[e, pair, here + a],
            wb.at[e, 0, here + ring(a, 3)], wb.at[e, 1, here + ring(a, 1)],
        )[op]
        to = next_a if op % 2 == 0 else prev_a
        return remote(ref, ref, l_send.at[k, op], l_recv.at[k, op], to)

    def line_in(k, op):
        e, here = k, 4 * b
        ref = (
            wb.at[e, pair, here + ring(a, 3)], wb.at[e, pair, here + ring(a, 1)],
            wb.at[e, 0, here + ring(a, 2)], wb.at[e, 1, here + ring(a, 2)],
        )[op]
        return remote(ref, ref, l_send.at[k, op], l_recv.at[k, op], next_a)

    def block(k, core, d):
        return wb.at[k, core, pl.ds(4 * ring(b, d), 4)]

    def plane(k, op):
        ref = block(k, (0, 1, 0, 1, 0, 1)[op], (0, 0, 0, 0, 3, 1)[op])
        to = right if op in (0, 1, 4) else left
        return remote(ref, ref, m_send.at[k, op], m_recv.at[k, op], to)

    def plane_in(k, op):
        ref = block(k, (0, 1, 0, 1, 0, 1)[op], (3, 3, 1, 1, 2, 2)[op])
        return remote(ref, ref, m_send.at[k, op], m_recv.at[k, op], left)

    def line_start(k):
        for core in range(2):
            shard_in(4 - k, core).wait_recv()
        line(k, 0).start()
        line(k, 1).start()

    def line_onward(k):
        line_in(k, 0).wait_recv()
        line(k, 2).start()
        line_in(k, 1).wait_recv()
        line(k, 3).start()

    def plane_start(k):
        line_in(k, 2).wait_recv()
        line_in(k, 3).wait_recv()
        for op in (0, 3, 1, 2):
            plane(k, op).start()

    def plane_onward(k):
        plane_in(k, 0).wait_recv()
        plane(k, 4).start()
        plane_in(k, 3).wait_recv()
        plane(k, 5).start()

    def plane_wait(k):
        for op in (1, 2, 4, 5):
            plane_in(k, op).wait_recv()

    def gather(d, i, way):
        j = tile(ring(a, 4 - d), b)
        ref = (kb, vt)[i].at[j]
        to = right if way == 0 else left
        return remote(ref, ref, g_send.at[0, d, i, way], g_recv.at[0, d, i, way], to)

    def gather_in(d, i, way):
        j = tile(ring(a, 4 - d), ring(b, 3 if way == 0 else 1))
        ref = (kb, vt)[i].at[j]
        return remote(ref, ref, g_send.at[0, d, i, way], g_recv.at[0, d, i, way], left)

    def onward(d, i):
        j = tile(ring(a, 4 - d), ring(b, 3 if FAR[i] == 0 else 1))
        ref = (kb, vt)[i].at[j]
        to = right if FAR[i] == 0 else left
        return remote(ref, ref, g_send.at[1, d, i, 0], g_recv.at[1, d, i, 0], to)

    def onward_in(d, i):
        ref = (kb, vt)[i].at[tile(ring(a, 4 - d), ring(b, 2))]
        return remote(ref, ref, g_send.at[1, d, i, 0], g_recv.at[1, d, i, 0], left)

    def visit(d):
        i = ring(a, 4 - d)
        return remote(qt.at[i, top], qt.at[4 + i, top], z_send.at[d], z_recv.at[d], across)

    def pass_on(d):
        for i in range(2):
            for way in range(2):
                gather(d, i, way).start()

    own.wait()
    pass_on(0)

    @pl.when(z == 1)
    def _():
        visit(0).start()

    for copy in small_in:
        copy.wait()
    starts, ends, total = [], [], jnp.int32(0)
    for j in range(GENOMES):
        starts.append(total)
        total = total + lengths[j]
        ends.append(total)
    def bounds(index):
        low, high = jnp.zeros(index.shape, jnp.int32), jnp.zeros(index.shape, jnp.int32)
        for j in range(GENOMES):
            low = jnp.where(index == j, starts[j], low)
            high = jnp.where(index == j, ends[j], high)
        return low, high

    def inside(position, axis, limits):
        spot = position + iota((ROWS, HD) if axis == 0 else (HD, ROWS), axis)
        return (spot >= limits[0]) & (spot < limits[1])

    by_lane, by_row = bounds(iota((1, HD), 1)), bounds(iota((HD, 1), 0))

    @pl.loop(0, 16)
    def _(j):
        gk[j] = jnp.where(inside((16 * z + j) * ROWS, 0, by_lane), 0.0, NEVER).astype(jnp.bfloat16)

    @pl.loop(0, 8)
    def _(i):
        j = tile(lax.rem(i, 4), b) + 16 * jnp.where(i >= 4, 1, z)
        qt[i, HD:] = jnp.where(inside(j * ROWS, 1, by_row), 1.0, 0.0).astype(jnp.bfloat16)

    mst[...] = jnp.full(mst.shape, START, jnp.float32)
    lst[...] = jnp.zeros(lst.shape, jnp.float32)
    acc[...] = jnp.zeros(acc.shape, jnp.float32)

    for d in (1, 3, 2):
        spread_in(d, 2).wait_recv()

        @pl.when(z == 1)
        def _():
            visit(d).start()

    shards_start()
    for d in (1, 3, 2):
        spread_in(d, 0).wait_recv()
        spread_in(d, 1).wait_recv()
        pass_on(d)

    slots = [tile(i, b) for i in range(4)]

    def fetch(n):
        near, far = (n >= 4) & (n < 12), (n >= 12) & (n < 16)
        d = jnp.where(near, n // 2 - 2, jnp.where(far, n - 12, 0))
        side = jnp.where(near, 3 - 2 * lax.rem(n, 2), jnp.where(far, 2, 0))
        j = step_tile(n)

        @pl.when((z == 0) & (n > 0) & (n < 5))
        def _():
            ref = qt.at[3 + n, top]
            remote(
                ref, ref, z_send.at[0], z_recv.at[ring(a, 5 - n)], across
            ).wait_recv()

        @pl.when(near & (side == 3))
        def _():
            for i in range(2):
                gather_in(d, i, 0).wait_recv()
                if FAR[i] == 0:
                    onward(d, i).start()

        @pl.when(near & (side == 1))
        def _():
            for i in range(2):
                gather_in(d, i, 1).wait_recv()
                if FAR[i] == 1:
                    onward(d, i).start()

        @pl.when(far)
        def _():
            onward_in(d, 0).wait_recv()
            onward_in(d, 1).wait_recv()

        return plan(n, j)

    def plan(n, j):
        same, prior = n == 16, n == 17
        ks = [
            jnp.where(same, slots[i], jnp.where(prior, jnp.maximum(slots[i] - 1, 0), j))
            for i in range(4)
        ]
        ss = [
            jnp.where(
                prior & (slots[i] == 0), 8, i + 4 * jnp.where(same | prior | (j > slots[i]), 1, 0)
            )
            for i in range(4)
        ]
        return j, ks, ss

    def score(k, s, buf, i):
        q = jnp.minimum(s, 7)
        wide_k = jnp.concatenate([kb[k], gk[k]], axis=1)
        buf[i] = jnp.dot(wide_k, qt[q], preferred_element_type=jnp.float32)

    def weigh(k, s, buf, i):
        scores, old = buf[i], mst[s]
        new = jnp.maximum(old, jnp.max(scores, axis=0, keepdims=True))
        exps = jnp.exp2(scores * LOG2 - new[0:1] * LOG2)
        fade = jnp.exp2((old - new) * LOG2)
        mst[s] = new
        lst[s] = lst[s] * fade + jnp.sum(exps.reshape(ROWS // 8, 8, ROWS), axis=0)
        acc[s] = acc[s] * fade[0:1] + jnp.dot(
            vt[k], exps.astype(jnp.bfloat16), preferred_element_type=jnp.float32
        )

    def causal(n, buf):
        @pl.when(n < 4)
        def _():
            ahead = iota((ROWS, ROWS), 0) <= iota((ROWS, ROWS), 1)
            buf[n] = jnp.where(ahead, buf[n], NEVER)

    def step(n, buf, following):
        _, ks_next, ss_next = fetch(jnp.minimum(n + 1, 17))
        for act, times in CONTROL.items():
            act = {"ls": line_start, "lo": line_onward, "ps": plane_start}[act]
            for k in times:

                @pl.when(n == times[k])
                def _():
                    act(k)

        _, ks, ss = plan(n, step_tile(n))
        for i in range(4):
            score(ks_next[i], ss_next[i], following, i)
            weigh(ks[i], ss[i], buf, i)
        causal(n + 1, following)

    def step_tile(n):
        near, far = (n >= 4) & (n < 12), (n >= 12) & (n < 16)
        d = jnp.where(near, n // 2 - 2, jnp.where(far, n - 12, 0))
        side = jnp.where(near, 3 - 2 * lax.rem(n, 2), jnp.where(far, 2, 0))
        own_line = jnp.where(n < 4, n, 3)
        return tile(jnp.where(near | far, ring(a, 4 - d), own_line), ring(b, side))

    @pl.when(z == 1)
    def _():
        qt[4:8, 0:HD] = jnp.zeros((4, HD, ROWS), jnp.bfloat16)

    _, first_ks, first_ss = plan(jnp.int32(0), tile(0, b))
    for i in range(4):
        score(first_ks[i], first_ss[i], even, i)
    causal(jnp.int32(0), even)

    @pl.loop(0, 9)
    def _(n):
        step(2 * n, even, odd)
        step(2 * n + 1, odd, even)

    def give(i):
        return [
            remote(oth.at[0, i], oth.at[1, i], r_send.at[0, i], r_recv.at[0, i], across),
            remote(ost.at[0, i], ost.at[1, i], r_send.at[1, i], r_recv.at[1, i], across),
        ]

    def close(i):
        total = jnp.sum(lst[i], axis=0, keepdims=True)
        return total, acc[i] * (1.0 / jnp.maximum(total, 1.0e-30))

    base = c * ROWS
    tail = remote(
        prod.at[:, pl.ds(ROWS, 128)], prod.at[:, pl.ds(0, 128)], h_send.at[1], h_recv.at[1], after
    )

    def featurize():
        streams_in.wait()
        halo.wait_recv()
        spot = base + iota((ROWS, HD), 0)
        first = jnp.zeros((ROWS, HD), jnp.int32)
        for j in range(1, GENOMES):
            first = jnp.where(spot >= starts[j], starts[j], first)
        depth = spot - first

        @pl.loop(0, 4)
        def _(n):
            lanes = pl.ds(pl.multiple_of(n * HD, HD), HD)
            made = []
            for j in range(3):
                data = sb[j, :, lanes].astype(jnp.float32)
                taps = short[j, :, lanes].astype(jnp.float32)
                total = data[16:] * taps[0:1]
                for lag in range(1, SHORT):
                    moved = pltpu.roll(data, lag, 0)[16:]
                    total = total + jnp.where(depth >= lag, moved * taps[lag : lag + 1], 0.0)
                made.append(total.astype(jnp.bfloat16))
            f0[n] = made[0]
            prod[n, pl.ds(128, ROWS)] = (
                made[1].astype(jnp.float32) * made[2].astype(jnp.float32)
            ).astype(jnp.bfloat16)
        tail.start()

    def chores():
        line_start(2)
        for k in (1, 3):
            if k not in CONTROL["lo"]:
                line_onward(k)
        for k in (1, 3):
            if k not in CONTROL["ps"]:
                plane_start(k)
        featurize()
        line_onward(2)
        if EARLY:
            plane_start(2)
        plane_onward(1)

    def home(d):
        to_a = ring(a, d)
        return remote(ob.at[to_a], att.at[0, p, a], o_send.at[d], o_recv.at[d], dev(to_a, b))

    def home_in(d):
        ref = att.at[0, p, ring(a, 4 - d)]
        return remote(ref, ref, o_send.at[d], o_recv.at[d], dev(ring(a, 4 - d), b))

    if "ls" not in CONTROL:
        for k in (1, 3):
            line_start(k)

    @pl.when(z == 1)
    def _():
        chores()

    for d in (1, 2, 3, 0):
        i = ring(a, d)
        total, out = close(i)
        ob[i] = out.T.astype(jnp.bfloat16)

        @pl.when(z == 1)
        def _():
            for copy in give(i):
                copy.wait_recv()
            m_other, l_other = ost[1, i, 0, 0:1], ost[1, i, 1, 0:1]
            m_own = mst[i, 0:1]
            top = jnp.maximum(m_own, m_other)
            w_own = jnp.exp2((m_own - top) * LOG2) * total
            w_other = jnp.exp2((m_other - top) * LOG2) * l_other
            share = 1.0 / (w_own + w_other)
            both = out * (w_own * share) + oth[1, i].astype(jnp.float32) * (w_other * share)
            ob[i] = both.T.astype(jnp.bfloat16)

        if d > 0:
            home(d).start()
        else:
            att[0, p, a] = ob[i]

    up, down = (c, lax.rem(t + 2, 8)), (c, lax.rem(t + 6, 8))
    halves = (pl.ds(0, 2), pl.ds(2, 2))

    def climb(op):
        half = (0, 1, 0, 1, 0, 1)[op]
        src = (0, 0, 0, 0, 3, 1)[op]
        dst = (3, 3, 1, 1, 2, 2)[op]
        to = up if op in (0, 1, 4) else down
        return remote(
            att.at[src, p, halves[half]], att.at[dst, p, halves[half]],
            p_send.at[op], p_recv.at[op], to,
        )

    def climb_in(op):
        ref = att.at[(3, 3, 1, 1, 2, 2)[op], p, halves[op % 2]]
        return remote(ref, ref, p_send.at[op], p_recv.at[op], up)

    def cross(op):
        ref = att.at[0, p] if op == 6 else att.at[(3, 3, 1, 1, 2, 2)[op], p, halves[op % 2]]
        return remote(ref, ref, n_send.at[op], n_recv.at[op], sibling)

    def cross_in(op):
        q = 1 - p
        ref = att.at[0, q] if op == 6 else att.at[(3, 3, 1, 1, 2, 2)[op], q, halves[op % 2]]
        return remote(ref, ref, n_send.at[op], n_recv.at[op], sibling)

    def multiply(e):
        rows = jnp.concatenate([att[e, core, i] for core in range(2) for i in range(4)], axis=1)

        @pl.loop(0, 2)
        def _(n):
            lanes = pl.ds(pl.multiple_of(n * 512, 512), 512)
            w = wb[e, :, :, :, lanes].reshape(1024, 512)
            sums[:, lanes] += jnp.dot(rows, w, preferred_element_type=jnp.float32)

    flip = jnp.where(
        lax.rem(iota((128, 128), 0) + iota((128, 128), 1), 128) == 0, 1.0, 0.0
    ).astype(jnp.bfloat16)
    taps_back = jnp.dot(medium[...], flip, preferred_element_type=jnp.float32)
    hyo_taps = taps_back

    def genome_at(position):
        genome = jnp.zeros(position.shape, jnp.int32)
        for j in range(GENOMES):
            genome = genome + jnp.where(position >= ends[j], 1, 0)
        return genome

    taps_ref[...] = hyo_taps.reshape(4, 8, 128)

    def convolve(n):
        lt, blk = n // 2, lax.rem(n, 2)
        here = base + blk * 128
        rows, cols = iota((128, 128), 0), iota((128, 128), 1)
        genome_now = genome_at(here + rows)
        genome_src = genome_at(here + cols)
        earlier = here - 128 + cols
        genome_prev = genome_at(earlier)
        near = (genome_now == genome_src) & (rows >= cols)
        far = (genome_now == genome_prev) & (rows < cols) & (earlier >= 0)
        data = prod[lt, pl.ds(pl.multiple_of(blk * 128, 128), 256)]
        band = iota((128, 128), 1) // 16
        out = jnp.zeros((128, 128), jnp.float32)
        for g in range(8):
            taps = jnp.broadcast_to(taps_ref[lt, g : g + 1], (128, 128))
            around = pltpu.roll(taps, 0, 1, stride=1, stride_axis=0)
            weights = jnp.concatenate(
                [jnp.where(far, around, 0.0), jnp.where(near, around, 0.0)], axis=1
            ).astype(jnp.bfloat16)
            term = jnp.dot(weights, data, preferred_element_type=jnp.float32)
            out = jnp.where(band == g, term, out)
        place = pl.ds(pl.multiple_of(blk * 128, 128), 128)
        hyo[lt, place] = (f0[lt, place].astype(jnp.float32) * out).astype(jnp.bfloat16)

    @pl.when(z == 0)
    def _():
        for i in range(4):
            total, out = close(4 + i)
            oth[0, i] = out.astype(jnp.bfloat16)
            ost[0, i, 0] = mst[4 + i]
            ost[0, i, 1] = jnp.broadcast_to(total, (8, ROWS))
            for copy in give(i):
                copy.start()

    @pl.when(z == 0)
    def _():
        chores()

    for d in (1, 2, 3):
        home_in(d).wait_recv()
    for op in (0, 3, 1, 2):
        climb(op).start()
    cross(6).start()
    attended_out = [
        pltpu.make_async_copy(att.at[0, p, i], head(attended, i), lo_sem.at[6 + i]) for i in range(4)
    ]
    for copy in attended_out:
        copy.start()
    residual_in.wait()
    sums[...] = res[...].astype(jnp.float32)
    if not EARLY:
        plane_start(2)
    tail.wait_recv()

    @pl.loop(0, 4)
    def _(n):
        convolve(n)

    plane_onward(3)
    climb_in(0).wait_recv()
    climb(4).start()
    cross(0).start()
    climb_in(3).wait_recv()
    climb(5).start()
    cross(3).start()

    plane_onward(2)

    @pl.loop(4, 8)
    def _(n):
        convolve(n)

    hyena_out = [
        pltpu.make_async_copy(hyo.at[i], head(hyena, i), lo_sem.at[i]) for i in range(4)
    ]
    for copy in hyena_out:
        copy.start()
    weights_in.wait()
    cross_in(6).wait_recv()
    remote(wb.at[0, 1 - p], wb.at[0, 1 - p], w_send.at[0], w_recv.at[0], sibling).wait_recv()
    multiply(0)
    for op in (1, 2):
        climb_in(op).wait_recv()
        cross(op).start()
    for d in (1, 2, 3):
        for i in range(3):
            spread(d, i).wait_send()
        home(d).wait_send()
        for core in range(2):
            shard(d, core).wait_send()
        for op in range(4):
            line(d, op).wait_send()
    halo.wait_send()
    tail.wait_send()
    swap.wait_send()
    for d in range(4):
        for i in range(2):
            for way in range(2):
                gather(d, i, way).wait_send()
            onward(d, i).wait_send()

    @pl.when(z == 1)
    def _():
        for d in range(4):
            visit(d).wait_send()

    @pl.when(z == 0)
    def _():
        for i in range(4):
            for copy in give(i):
                copy.wait_send()

    for copy in hyena_out + attended_out:
        copy.wait()
    for e, ops in ((1, (2, 3)), (3, (0, 1)), (2, (4, 5))):
        if e == 2:
            for op in ops:
                climb_in(op).wait_recv()
                cross(op).start()
        plane_wait(e)
        for op in ops:
            cross_in(op).wait_recv()
        if e != 2:
            multiply(e)
    rows = jnp.concatenate([att[2, core, i] for core in range(2) for i in range(4)], axis=1)
    mixed_out = []
    for n in range(2):
        lanes = slice(n * 512, (n + 1) * 512)
        w = wb[2, :, :, :, lanes].reshape(1024, 512)
        mix[:, lanes] = (
            sums[:, lanes] + jnp.dot(rows, w, preferred_element_type=jnp.float32)
        ).astype(jnp.bfloat16)
        mixed_out.append(pltpu.make_async_copy(mix.at[:, lanes], mixed.at[:, lanes], lo_sem.at[4 + n]))
        mixed_out[n].start()

    for d in (1, 2, 3):
        for op in range(6):
            plane(d, op).wait_send()
    for op in range(6):
        climb(op).wait_send()
    for op in range(7):
        cross(op).wait_send()
    for copy in mixed_out:
        copy.wait()


def hand_out(a_in, b_in, c_in, a_out, b_out, c_out, a_mid, b_mid, c_mid, sem):
    parts = [
        (src.at[rows], mid.at[rows], dst.at[rows], sem.at[n, i])
        for n, (src, mid, dst) in enumerate(
            ((a_in, a_mid, a_out), (b_in, b_mid, b_out), (c_in, c_mid, c_out))
        )
        for i, rows in enumerate((pl.ds(0, 128), pl.ds(128, 128)))
    ]
    first = [pltpu.make_async_copy(src, mid, s.at[0]) for src, mid, _, s in parts]
    second = [pltpu.make_async_copy(mid, dst, s.at[1]) for _, mid, dst, s in parts]
    for copy in first:
        copy.start()
    for one, two in zip(first, second):
        one.wait()
        two.start()
    for copy in second:
        copy.wait()


def body(residual, streams, short_filter, medium_filter, queries, keys, values, lengths, w_out):
    bf16, f32 = jnp.bfloat16, jnp.float32
    anywhere = pl.BlockSpec(memory_space=pl.ANY)
    dma = pltpu.SemaphoreType.DMA
    scratch = [
        pltpu.SMEM((GENOMES,), jnp.int32),
        pltpu.VMEM((3, SHORT, 512), bf16),
        pltpu.VMEM((32, 128), bf16),
        pltpu.VMEM((2, ROWS, 512), bf16),
        pltpu.VMEM((4, HD, ROWS), bf16),
        pltpu.VMEM((4, HD, ROWS), bf16),
        pltpu.VMEM((8, 2 * HD, ROWS), bf16),
        pltpu.VMEM((4, ROWS, ROWS), f32),
        pltpu.VMEM((4, ROWS, ROWS), f32),
        pltpu.VMEM((16, ROWS, HD), bf16),
        pltpu.VMEM((16, HD, ROWS), bf16),
        pltpu.VMEM((16, ROWS, HD), bf16),
        pltpu.VMEM((9, 8, ROWS), f32),
        pltpu.VMEM((9, 8, ROWS), f32),
        pltpu.VMEM((9, HD, ROWS), f32),
        pltpu.VMEM((2, 4, HD, ROWS), bf16),
        pltpu.VMEM((2, 4, 2, 8, ROWS), f32),
        pltpu.VMEM((4, ROWS, HD), bf16),
        pltpu.VMEM((4, 2, 4, ROWS, HD), bf16),
        pltpu.VMEM((4, 2, 16, 32, COLS), bf16),
        pltpu.VMEM((ROWS, COLS), f32),
        pltpu.VMEM((ROWS, COLS), bf16),
        pltpu.VMEM((ROWS, COLS), bf16),
        pltpu.VMEM((4, 8, 128), f32),
        pltpu.VMEM((3, ROWS + 16, 512), bf16),
        pltpu.VMEM((4, ROWS, HD), bf16),
        pltpu.VMEM((4, ROWS + 128, HD), bf16),
        pltpu.VMEM((4, ROWS, HD), bf16),
        dma((16,)),
        dma((4, 3)), dma((4, 3)),
        dma((2, 4, 2, 2)), dma((2, 4, 2, 2)),
        dma((2,)), dma((2,)),
        dma((4,)), dma((4,)),
        dma((2, 4)), dma((2, 4)),
        dma((4,)), dma((4,)),
        dma((1,)), dma((1,)),
        dma((4, 2)), dma((4, 2)),
        dma((4, 4)), dma((4, 4)),
        dma((4, 6)), dma((4, 6)),
        dma((6,)), dma((6,)),
        dma((7,)), dma((7,)),
    ]
    made = pl.pallas_call(
        kernel,
        out_shape=(
            jax.ShapeDtypeStruct((ROWS, 512), bf16),
            jax.ShapeDtypeStruct((ROWS, 512), bf16),
            jax.ShapeDtypeStruct((ROWS, COLS), bf16),
        ),
        in_specs=[anywhere] * 9,
        out_specs=(anywhere, anywhere, anywhere),
        scratch_shapes=scratch,
        compiler_params=pltpu.CompilerParams(
            collective_id=0, has_side_effects=True, vmem_limit_bytes=56 * 1024 * 1024
        ),
        cost_estimate=pl.CostEstimate(
            flops=7_000_000_000, bytes_accessed=16_000_000, transcendentals=5_000_000
        ),
        name="mixer",
    )(
        lengths, residual, jnp.transpose(streams, (1, 0, 2)), jnp.transpose(short_filter, (1, 0, 2)),
        medium_filter.T, queries, keys, values, w_out.reshape(16, 32, 8192),
    )
    return pl.pallas_call(
        hand_out,
        out_shape=tuple(jax.ShapeDtypeStruct(v.shape, v.dtype) for v in made),
        in_specs=[anywhere] * 3,
        out_specs=(anywhere,) * 3,
        scratch_shapes=[pltpu.VMEM(v.shape, v.dtype) for v in made] + [dma((3, 2, 2))],
        name="hand_out",
    )(*made)


def solution(mesh):
    in_specs = (
        P("ctx", "tp"),
        P("ctx", None, "tp"),
        P(None, None, "tp"),
        P(None, "tp"),
        P("ctx", "tp"),
        P("ctx", "tp"),
        P("ctx", "tp"),
        P(),
        P("tp", None),
    )
    out_specs = (P("ctx", "tp"), P("ctx", "tp"), P("ctx", "tp"))
    return jax.shard_map(body, mesh=mesh, in_specs=in_specs, out_specs=out_specs, check_vma=False)
```

time: 91.2 us -> 76.2 us (0.84)
  the two profiles are of different devices: /device:TPU:32 before, /device:TPU:1 now
where the time goes in v2:
time: 76.2 us; the launch traced here: 76.1 us
  Pallas kernels  75.4 us (99%)
    pallas_call x1, Pallas kernels, body(): pl.pallas_call(kernel, out_shape=(jax.ShapeDtypeStruct((ROWS, 512), bf16)...  73.3 us
    pallas_call x1, Pallas kernels, body(): pl.pallas_call(hand_out, out_shape=tuple((jax.ShapeDtypeStruct(v.shape, v...  2.1 us

profile of v2, /device:TPU:1, one launch (start us, length us, event | category | flops | bytes accessed | tf_op | source)
XLA Modules:
  0.0 76.1 jit_solution(5746089306055453006)
XLA Ops:
  0.6 73.3 %mixer.1 = (bf16[256,512]{1,0:T(8,128)(2,1)}, bf16[256,512]{1,0:T(8,128)(2,1)}, bf16[256,1024]{1,0:T(8,128)(2,1)}) custom-call(s32[8]{0:T(128)} %lengths_in.1, bf16[256,1024]{1,0:T(8,128)(2,1)} %residual.1, bf16[3,256,512]{2,1,0:T(8,128)(2,1)} %bitcast.5, bf16[3,7,512]{2,1,0:T(8,128)(2,1)} %bitcast.6, bf16[32,128]{1,0:T(8,128)(2,1)} %bitcast.7, ...), custom_call_target="tpu_custom_call" | custom-call | flops 7000000000 | bytes 16000000 | tf_op jit(solution)/shard_map/mixer/pallas_call | solution.py:761
  74.0 2.1 %hand_out.1 = (bf16[256,512]{1,0:T(8,128)(2,1)}, bf16[256,512]{1,0:T(8,128)(2,1)}, bf16[256,1024]{1,0:T(8,128)(2,1)}) custom-call(bf16[256,512]{1,0:T(8,128)(2,1)} %get-tuple-element.6.a_in, bf16[256,512]{1,0:T(8,128)(2,1)} %get-tuple-element.7.b_in, bf16[256,1024]{1,0:T(8,128)(2,1)} %get-tuple-element.8.c_in), custom_call_target="tpu_custom_call" | custom-call | tf_op jit(solution)/shard_map/hand_out/pallas_call | solution.py:782

commit v3 on v2

--- a/solution.py
+++ b/solution.py
@@ -19,8 +19,7 @@
 LOG2 = math.log2(math.e) / math.sqrt(HD)
 MESH = pl.DeviceIdType.MESH
 FAR = (0, 1)
-EARLY = False
-CONTROL = {"ls": {1: 8, 3: 9}, "lo": {1: 15, 3: 16}, "ps": {}}
+LINES = ((8, 1, True), (9, 3, True), (15, 1, False), (16, 3, False))
 
 
 def iota(shape, axis):
@@ -110,12 +109,12 @@
         to_a = ring(a, d)
         src = (head(keys, to_a), tv.at[to_a], tq.at[to_a])[i]
         dst = (kb.at[me], vt.at[me], qt.at[a, top])[i]
-        return remote(src, dst, a_send.at[d, i], a_recv.at[d, i], dev(to_a, b))
+        return remote(src, dst, a_send.at[d - 1, i], a_recv.at[d - 1, i], dev(to_a, b))
 
     def spread_in(d, i):
         from_a = ring(a, 4 - d)
         dst = (kb.at[tile(from_a, b)], vt.at[tile(from_a, b)], qt.at[from_a, top])[i]
-        return remote(dst, dst, a_send.at[d, i], a_recv.at[d, i], dev(from_a, b))
+        return remote(dst, dst, a_send.at[d - 1, i], a_recv.at[d - 1, i], dev(from_a, b))
 
     for i in (2, 0, 1):
         for d in (1, 3, 2):
@@ -133,12 +132,12 @@
         to = lax.rem(2 * zh + 2 * d, 8) + core
         return remote(
             block_cols(to, spot), wb.at[4 - d, p, spot],
-            s_send.at[d, core], s_recv.at[d, p], (c, to),
+            s_send.at[d - 1, core], s_recv.at[d - 1, p], (c, to),
         )
 
     def shard_in(d, core):
         ref = wb.at[4 - d, core, 4 * b + a]
-        return remote(ref, ref, s_send.at[d, core], s_recv.at[d, core], sibling)
+        return remote(ref, ref, s_send.at[d - 1, core], s_recv.at[d - 1, core], sibling)
 
     for d in (3, 1):
         for core in range(2):
@@ -160,7 +159,7 @@
             wb.at[e, 0, here + ring(a, 3)], wb.at[e, 1, here + ring(a, 1)],
         )[op]
         to = next_a if op % 2 == 0 else prev_a
-        return remote(ref, ref, l_send.at[k, op], l_recv.at[k, op], to)
+        return remote(ref, ref, l_send.at[k - 1, op], l_recv.at[k - 1, op], to)
 
     def line_in(k, op):
         e, here = k, 4 * b
@@ -168,7 +167,7 @@
             wb.at[e, pair, here + ring(a, 3)], wb.at[e, pair, here + ring(a, 1)],
             wb.at[e, 0, here + ring(a, 2)], wb.at[e, 1, here + ring(a, 2)],
         )[op]
-        return remote(ref, ref, l_send.at[k, op], l_recv.at[k, op], next_a)
+        return remote(ref, ref, l_send.at[k - 1, op], l_recv.at[k - 1, op], next_a)
 
     def block(k, core, d):
         return wb.at[k, core, pl.ds(4 * ring(b, d), 4)]
@@ -176,11 +175,11 @@
     def plane(k, op):
         ref = block(k, (0, 1, 0, 1, 0, 1)[op], (0, 0, 0, 0, 3, 1)[op])
         to = right if op in (0, 1, 4) else left
-        return remote(ref, ref, m_send.at[k, op], m_recv.at[k, op], to)
+        return remote(ref, ref, m_send.at[k - 1, op], m_recv.at[k - 1, op], to)
 
     def plane_in(k, op):
         ref = block(k, (0, 1, 0, 1, 0, 1)[op], (3, 3, 1, 1, 2, 2)[op])
-        return remote(ref, ref, m_send.at[k, op], m_recv.at[k, op], left)
+        return remote(ref, ref, m_send.at[k - 1, op], m_recv.at[k - 1, op], left)
 
     def line_start(k):
         for core in range(2):
@@ -214,22 +213,22 @@
         j = tile(ring(a, 4 - d), b)
         ref = (kb, vt)[i].at[j]
         to = right if way == 0 else left
-        return remote(ref, ref, g_send.at[0, d, i, way], g_recv.at[0, d, i, way], to)
+        return remote(ref, ref, g_send.at[d, 2 * i + way], g_recv.at[d, 2 * i + way], to)
 
     def gather_in(d, i, way):
         j = tile(ring(a, 4 - d), ring(b, 3 if way == 0 else 1))
         ref = (kb, vt)[i].at[j]
-        return remote(ref, ref, g_send.at[0, d, i, way], g_recv.at[0, d, i, way], left)
+        return remote(ref, ref, g_send.at[d, 2 * i + way], g_recv.at[d, 2 * i + way], left)
 
     def onward(d, i):
         j = tile(ring(a, 4 - d), ring(b, 3 if FAR[i] == 0 else 1))
         ref = (kb, vt)[i].at[j]
         to = right if FAR[i] == 0 else left
-        return remote(ref, ref, g_send.at[1, d, i, 0], g_recv.at[1, d, i, 0], to)
+        return remote(ref, ref, g_send.at[d, 4 + i], g_recv.at[d, 4 + i], to)
 
     def onward_in(d, i):
         ref = (kb, vt)[i].at[tile(ring(a, 4 - d), ring(b, 2))]
-        return remote(ref, ref, g_send.at[1, d, i, 0], g_recv.at[1, d, i, 0], left)
+        return remote(ref, ref, g_send.at[d, 4 + i], g_recv.at[d, 4 + i], left)
 
     def visit(d):
         i = ring(a, 4 - d)
@@ -367,13 +366,11 @@
 
     def step(n, buf, following):
         _, ks_next, ss_next = fetch(jnp.minimum(n + 1, 17))
-        for act, times in CONTROL.items():
-            act = {"ls": line_start, "lo": line_onward, "ps": plane_start}[act]
-            for k in times:
-
-                @pl.when(n == times[k])
-                def _():
-                    act(k)
+        for when, k, starts_line in LINES:
+
+            @pl.when(n == when)
+            def _():
+                (line_start if starts_line else line_onward)(k)
 
         _, ks, ss = plan(n, step_tile(n))
         for i in range(4):
@@ -444,35 +441,28 @@
             ).astype(jnp.bfloat16)
         tail.start()
 
-    def chores():
+    def spread_weights():
         line_start(2)
         for k in (1, 3):
-            if k not in CONTROL["lo"]:
-                line_onward(k)
-        for k in (1, 3):
-            if k not in CONTROL["ps"]:
-                plane_start(k)
+            plane_start(k)
+
+    def chores():
+        spread_weights()
         featurize()
         line_onward(2)
-        if EARLY:
-            plane_start(2)
-        plane_onward(1)
 
     def home(d):
         to_a = ring(a, d)
-        return remote(ob.at[to_a], att.at[0, p, a], o_send.at[d], o_recv.at[d], dev(to_a, b))
+        return remote(ob.at[to_a], att.at[0, p, a], o_send.at[d - 1], o_recv.at[d - 1], dev(to_a, b))
 
     def home_in(d):
         ref = att.at[0, p, ring(a, 4 - d)]
-        return remote(ref, ref, o_send.at[d], o_recv.at[d], dev(ring(a, 4 - d), b))
-
-    if "ls" not in CONTROL:
-        for k in (1, 3):
-            line_start(k)
+        return remote(ref, ref, o_send.at[d - 1], o_recv.at[d - 1], dev(ring(a, 4 - d), b))
 
     @pl.when(z == 1)
     def _():
         chores()
+        plane_onward(1)
 
     for d in (1, 2, 3, 0):
         i = ring(a, d)
@@ -596,8 +586,11 @@
         copy.start()
     residual_in.wait()
     sums[...] = res[...].astype(jnp.float32)
-    if not EARLY:
-        plane_start(2)
+    @pl.when(z == 0)
+    def _():
+        plane_onward(1)
+
+    plane_start(2)
     tail.wait_recv()
 
     @pl.loop(0, 4)
@@ -623,13 +616,13 @@
     ]
     for copy in hyena_out:
         copy.start()
+    for op in (1, 2):
+        climb_in(op).wait_recv()
+        cross(op).start()
     weights_in.wait()
     cross_in(6).wait_recv()
     remote(wb.at[0, 1 - p], wb.at[0, 1 - p], w_send.at[0], w_recv.at[0], sibling).wait_recv()
     multiply(0)
-    for op in (1, 2):
-        climb_in(op).wait_recv()
-        cross(op).start()
     for d in (1, 2, 3):
         for i in range(3):
             spread(d, i).wait_send()
@@ -661,25 +654,29 @@
     for copy in hyena_out + attended_out:
         copy.wait()
     for e, ops in ((1, (2, 3)), (3, (0, 1)), (2, (4, 5))):
-        if e == 2:
-            for op in ops:
-                climb_in(op).wait_recv()
-                cross(op).start()
         plane_wait(e)
         for op in ops:
             cross_in(op).wait_recv()
+        if e == 1:
+            for op in (4, 5):
+                climb_in(op).wait_recv()
+                cross(op).start()
         if e != 2:
             multiply(e)
     rows = jnp.concatenate([att[2, core, i] for core in range(2) for i in range(4)], axis=1)
     mixed_out = []
-    for n in range(2):
-        lanes = slice(n * 512, (n + 1) * 512)
-        w = wb[2, :, :, :, lanes].reshape(1024, 512)
+    for n in range(4):
+        lanes = slice(n * 256, (n + 1) * 256)
+        w = wb[2, :, :, :, lanes].reshape(1024, 256)
         mix[:, lanes] = (
             sums[:, lanes] + jnp.dot(rows, w, preferred_element_type=jnp.float32)
         ).astype(jnp.bfloat16)
-        mixed_out.append(pltpu.make_async_copy(mix.at[:, lanes], mixed.at[:, lanes], lo_sem.at[4 + n]))
-        mixed_out[n].start()
+        for m in range(2):
+            place = (pl.ds(m * 128, 128), lanes)
+            mixed_out.append(
+                pltpu.make_async_copy(mix.at[place], mixed.at[place], lo_sem.at[(4, 5, 13, 14, 15, 10, 11, 12)[2 * n + m]])
+            )
+            mixed_out[-1].start()
 
     for d in (1, 2, 3):
         for op in range(6):
@@ -745,16 +742,16 @@
         pltpu.VMEM((4, ROWS + 128, HD), bf16),
         pltpu.VMEM((4, ROWS, HD), bf16),
         dma((16,)),
-        dma((4, 3)), dma((4, 3)),
-        dma((2, 4, 2, 2)), dma((2, 4, 2, 2)),
+        dma((3, 3)), dma((3, 3)),
+        dma((4, 6)), dma((4, 6)),
         dma((2,)), dma((2,)),
         dma((4,)), dma((4,)),
         dma((2, 4)), dma((2, 4)),
         dma((4,)), dma((4,)),
         dma((1,)), dma((1,)),
-        dma((4, 2)), dma((4, 2)),
-        dma((4, 4)), dma((4, 4)),
-        dma((4, 6)), dma((4, 6)),
+        dma((3, 2)), dma((3, 2)),
+        dma((3, 4)), dma((3, 4)),
+        dma((3, 6)), dma((3, 6)),
         dma((6,)), dma((6,)),
         dma((7,)), dma((7,)),
     ]

time: 76.2 us -> 75.8 us (level)
  no operation moved by 1% of the time
where the time goes in v3:
time: 75.8 us; the launch traced here: 75.7 us
  Pallas kernels  75 us (99%)
    pallas_call x1, Pallas kernels, body(): pl.pallas_call(kernel, out_shape=(jax.ShapeDtypeStruct((ROWS, 512), bf16)...  72.9 us
    pallas_call x1, Pallas kernels, body(): pl.pallas_call(hand_out, out_shape=tuple((jax.ShapeDtypeStruct(v.shape, v...  2.1 us

profile of v3, /device:TPU:1, one launch (start us, length us, event | category | flops | bytes accessed | tf_op | source)
XLA Modules:
  0.0 75.7 jit_solution(14953024257254175683)
XLA Ops:
  0.6 72.9 %mixer.1 = (bf16[256,512]{1,0:T(8,128)(2,1)}, bf16[256,512]{1,0:T(8,128)(2,1)}, bf16[256,1024]{1,0:T(8,128)(2,1)}) custom-call(s32[8]{0:T(128)} %lengths_in.1, bf16[256,1024]{1,0:T(8,128)(2,1)} %residual.1, bf16[3,256,512]{2,1,0:T(8,128)(2,1)} %bitcast.5, bf16[3,7,512]{2,1,0:T(8,128)(2,1)} %bitcast.6, bf16[32,128]{1,0:T(8,128)(2,1)} %bitcast.7, ...), custom_call_target="tpu_custom_call" | custom-call | flops 7000000000 | bytes 16000000 | tf_op jit(solution)/shard_map/mixer/pallas_call | solution.py:758
  73.6 2.1 %hand_out.1 = (bf16[256,512]{1,0:T(8,128)(2,1)}, bf16[256,512]{1,0:T(8,128)(2,1)}, bf16[256,1024]{1,0:T(8,128)(2,1)}) custom-call(bf16[256,512]{1,0:T(8,128)(2,1)} %get-tuple-element.6.a_in, bf16[256,512]{1,0:T(8,128)(2,1)} %get-tuple-element.7.b_in, bf16[256,1024]{1,0:T(8,128)(2,1)} %get-tuple-element.8.c_in), custom_call_target="tpu_custom_call" | custom-call | tf_op jit(solution)/shard_map/hand_out/pallas_call | solution.py:779

commit v4 on v3

--- a/solution.py
+++ b/solution.py
@@ -576,7 +576,7 @@
 
     for d in (1, 2, 3):
         home_in(d).wait_recv()
-    for op in (0, 3, 1, 2):
+    for op in (0, 3):
         climb(op).start()
     cross(6).start()
     attended_out = [
@@ -597,6 +597,8 @@
     def _(n):
         convolve(n)
 
+    for op in (1, 2):
+        climb(op).start()
     plane_onward(3)
     climb_in(0).wait_recv()
     climb(4).start()

time: 75.8 us -> 75.8 us (level)
  no operation moved by 1% of the time
where the time goes in v4:
time: 75.8 us; the launch traced here: 75.7 us
  Pallas kernels  75 us (99%)
    pallas_call x1, Pallas kernels, body(): pl.pallas_call(kernel, out_shape=(jax.ShapeDtypeStruct((ROWS, 512), bf16)...  72.9 us
    pallas_call x1, Pallas kernels, body(): pl.pallas_call(hand_out, out_shape=tuple((jax.ShapeDtypeStruct(v.shape, v...  2.1 us

profile of v4, /device:TPU:1, one launch (start us, length us, event | category | flops | bytes accessed | tf_op | source)
XLA Modules:
  0.0 75.7 jit_solution(9848997170990574128)
XLA Ops:
  0.6 72.9 %mixer.1 = (bf16[256,512]{1,0:T(8,128)(2,1)}, bf16[256,512]{1,0:T(8,128)(2,1)}, bf16[256,1024]{1,0:T(8,128)(2,1)}) custom-call(s32[8]{0:T(128)} %lengths_in.1, bf16[256,1024]{1,0:T(8,128)(2,1)} %residual.1, bf16[3,256,512]{2,1,0:T(8,128)(2,1)} %bitcast.5, bf16[3,7,512]{2,1,0:T(8,128)(2,1)} %bitcast.6, bf16[32,128]{1,0:T(8,128)(2,1)} %bitcast.7, ...), custom_call_target="tpu_custom_call" | custom-call | flops 7000000000 | bytes 16000000 | tf_op jit(solution)/shard_map/mixer/pallas_call | solution.py:760
  73.6 2.1 %hand_out.1 = (bf16[256,512]{1,0:T(8,128)(2,1)}, bf16[256,512]{1,0:T(8,128)(2,1)}, bf16[256,1024]{1,0:T(8,128)(2,1)}) custom-call(bf16[256,512]{1,0:T(8,128)(2,1)} %get-tuple-element.6.a_in, bf16[256,512]{1,0:T(8,128)(2,1)} %get-tuple-element.7.b_in, bf16[256,1024]{1,0:T(8,128)(2,1)} %get-tuple-element.8.c_in), custom_call_target="tpu_custom_call" | custom-call | tf_op jit(solution)/shard_map/hand_out/pallas_call | solution.py:781
